TPU v7x, 256 devices: a whole 4x4x8 slice. The times are simulated.
256 devices in a mesh: gx: 8 (over z), gy: 4 (over y), gz: 8 (over x, core).
Axes of the slice: x: 4, y: 4, z: 8, core: 2. Of those that a mesh axis runs over, the one named last changes fastest.
Arguments:
- offsets: float32 [3, 1048576], P(None, ('gx', 'gy', 'gz')), may hold values from 0 to 1
- strength: float32 [3, 1048576], P(None, ('gx', 'gy', 'gz')), may hold values from -0.012 to 0.012
- ghost_list: int32 [393216], P(('gx', 'gy', 'gz')), may hold values from 0 to 4095
- pair_targets: int32 [32768], P(('gx', 'gy', 'gz')), may hold values from 0 to 31
- pair_sources: int32 [32768], P(('gx', 'gy', 'gz')), may hold values from 0 to 103
- owners: int32 [8192, 1], P(('gx', 'gy', 'gz')), may hold values from 0 to 31; in each aligned block of 32 rows (0 to 31, 32 to 63, ...) at most 2 rows name the same one
Outputs:
- moved_positions: float32 [16384, 3, 128], P(('gx', 'gy', 'gz'))
- moved_velocity: float32 [16384, 3, 128], P(('gx', 'gy', 'gz'))
Inputs may be any that keep to these rules, and one draw needn't show every extreme that they name: `owners`: among the 32 blocks of one domain no owner is named more than 2 times.
All inputs are finite; a program needn't handle non-finite values.
Results may differ from a plain program's by a relative error of at most 0.0003.
Values sent between devices are 32-bit elements; how exact they have to be, the bound alone decides.
A program may use at most 128 MiB of HBM per device.

v0:
```python
import functools
import math

import jax
import jax.numpy as jnp
import numpy as np
from jax import lax
from jax.experimental import pallas as pl
from jax.experimental.pallas import tpu as pltpu
from jax.sharding import PartitionSpec as P

SEG = 4096
ORDER = 5
GHOST = 1536
NPAIR = 128
CAP = 2
LANES = 128
TILES = SEG // LANES
GHOST_TILES = GHOST // LANES
SOURCES = TILES + 6 * GHOST_TILES
UNROLL = 16

core_sq = 0.0025
time_step = 0.1
bf16 = jnp.bfloat16
f32 = jnp.float32
MESH = pl.DeviceIdType.MESH

TRIPLES = [
    (i, j, d - i - j)
    for d in range(ORDER + 1)
    for i in range(d, -1, -1)
    for j in range(d - i, -1, -1)
]
PLACE = {triple: at for at, triple in enumerate(TRIPLES)}
COUNT = len(TRIPLES)
MESSAGE = 256


def factorial(triple):
    return float(math.prod(math.factorial(e) for e in triple))


def lowered(triple, axis, by=1):
    out = list(triple)
    out[axis] -= by
    return tuple(out)


def monomials(coords):
    made = {}
    for triple in TRIPLES:
        if sum(triple) == 0:
            made[triple] = None
        else:
            axis = next(a for a in range(3) if triple[a])
            below = made[lowered(triple, axis)]
            made[triple] = coords[axis] if below is None else below * coords[axis]
    return made


def derivatives(separation):
    rx, ry, rz = separation
    inverse = 1.0 / (rx * rx + ry * ry + rz * rz + core_sq)
    taylor = {(0, 0, 0): lax.sqrt(inverse)}
    for triple in TRIPLES[1:]:
        n = sum(triple)
        first, second = None, None
        for axis in range(3):
            if triple[axis] >= 1:
                term = separation[axis] * taylor[lowered(triple, axis)]
                first = term if first is None else first + term
            if triple[axis] >= 2:
                term = taylor[lowered(triple, axis, 2)]
                second = term if second is None else second + term
        total = first * (-(2.0 * n - 1.0) / n)
        if second is not None:
            total = total - second * ((n - 1.0) / n)
        taylor[triple] = total * inverse
    return {t: v if factorial(t) == 1.0 else v * factorial(t) for t, v in taylor.items()}


def split3(value):
    high = value.astype(bf16).astype(f32)
    rest = value - high
    middle = rest.astype(bf16).astype(f32)
    return high, middle, rest - middle


def halves(value):
    high = value.astype(bf16)
    return high, (value - high.astype(f32)).astype(bf16)


def kernel(
    sizes,
    offsets, strength, ghost_list, targets, target_row, sources, owners,
    out_pos, out_vel,
    own, ghost_out, ghost_in, target_feat, source_feat, source_str, contrib, partial,
    message, column_in, plane_in, gathered, turned, local, far_weights, block_out, block_in,
    ghost_send, ghost_recv, column_send, column_recv, plane_send, plane_recv, block_send, block_recv,
):
    wide, tall, deep = sizes
    plane = wide * tall
    gx, gy, gz = lax.axis_index("gx"), lax.axis_index("gy"), lax.axis_index("gz")
    rank = gx * tall + gy
    side = 1.0 / deep
    sub = lax.broadcasted_iota(jnp.int32, (8, LANES), 0)

    def along(d):
        return (gx, gy, lax.rem(gz + d, deep))

    def across(d):
        other = lax.rem(rank + d, plane)
        return (other // tall, lax.rem(other, tall), gz)

    barrier = pltpu.get_barrier_semaphore()

    def greet_column(d, c):
        pl.semaphore_signal(barrier, inc=1, device_id=along(d), device_id_type=MESH)
        return c

    def greet_plane(d, c):
        pl.semaphore_signal(barrier, inc=1, device_id=across(d), device_id_type=MESH)
        return c

    lax.fori_loop(1, deep, greet_column, 0)
    lax.fori_loop(1, plane, greet_plane, 0)

    position = (gx, gy, gz)
    slots = []
    for axis, count in enumerate((wide, tall, deep)):
        at = position[axis]
        up = tuple(p + 1 if i == axis else p for i, p in enumerate(position))
        down = tuple(p - 1 if i == axis else p for i, p in enumerate(position))
        step = side if axis == 2 else 1.0
        slots.append((axis, -step, at > 0, at < count - 1, up))
        slots.append((axis, step, at < count - 1, at > 0, down))

    scale = jnp.where(lax.broadcasted_iota(jnp.int32, (3, LANES), 0) == 2, side, 1.0)
    own[...] = jnp.zeros_like(own)
    for t in range(TILES):
        lanes = slice(t * LANES, (t + 1) * LANES)
        own[8 * t : 8 * t + 3, :] = (offsets[:, lanes] - 0.5) * scale
        own[8 * t + 3 : 8 * t + 6, :] = strength[:, lanes]

    def dense(row):
        return own[pl.ds(row, TILES, stride=8), :]

    dense_strength = [dense(3 + k) for k in range(3)]

    lane = lax.broadcasted_iota(jnp.int32, (4, plane), 1)
    shift = tall.bit_length() - 1
    source_x, source_y = lane >> shift, lane & (tall - 1)
    away_x, away_y = gx - source_x, gy - source_y
    is_far = jnp.maximum(jnp.abs(away_x), jnp.abs(away_y)) >= 3

    column = owners[...]
    rows_i = lax.broadcasted_iota(jnp.int32, (TILES, TILES), 0)
    cols_i = lax.broadcasted_iota(jnp.int32, (TILES, TILES), 1)
    column_f = jnp.broadcast_to(column.astype(f32), (TILES, TILES))
    row_f = jnp.sum(jnp.where(rows_i == cols_i, column_f, 0.0), axis=0, keepdims=True)
    earlier = jnp.where((column_f == row_f) & (rows_i < cols_i), 1.0, 0.0)
    slot_f = jnp.sum(earlier, axis=0, keepdims=True) * plane + row_f
    slot_rows = lax.broadcasted_iota(jnp.int32, (CAP * plane, TILES), 0).astype(f32)
    placer = jnp.where(slot_rows == slot_f, 1.0, 0.0).astype(bf16)
    placer = jnp.concatenate([placer, placer, placer], axis=1)

    def place(which, k, field):
        parts = jnp.concatenate([p.astype(bf16) for p in split3(field)], axis=0)
        placed = jnp.dot(placer, parts, preferred_element_type=f32)
        for r in range(CAP):
            rows = pl.ds(which * plane * 8 + 3 * r + k, plane, stride=8)
            block_out[rows, :] = placed[r * plane : (r + 1) * plane]

    def block_rows(which, o):
        return pl.ds(pl.multiple_of(which * plane * 8 + 8 * o, 8), 8)

    def block_copy(which, d):
        target = across(d)
        other = target[0] * tall + target[1]
        return pltpu.make_async_remote_copy(
            src_ref=block_out.at[block_rows(which, other)],
            dst_ref=block_in.at[block_rows(which, rank)],
            send_sem=block_send.at[which],
            recv_sem=block_recv.at[which],
            device_id=target,
            device_id_type=MESH,
        )

    def send_blocks(which):
        def send(d, c):
            block_copy(which, d).start()
            return c

        lax.fori_loop(1, plane, send, 0)
        block_in[block_rows(which, rank), :] = block_out[block_rows(which, rank), :]

    def all_blocks(which):
        rows = pl.ds(which * plane * 8, (plane - 1) * 8)
        return pltpu.make_async_remote_copy(
            src_ref=block_out.at[rows],
            dst_ref=block_in.at[rows],
            send_sem=block_send.at[which],
            recv_sem=block_recv.at[which],
            device_id=across(1),
            device_id_type=MESH,
        )

    def ghost_copy(step, j):
        return pltpu.make_async_remote_copy(
            src_ref=ghost_out.at[step],
            dst_ref=ghost_in.at[step, j],
            send_sem=ghost_send.at[step, j],
            recv_sem=ghost_recv.at[step, j],
            device_id=slots[j][4],
            device_id_type=MESH,
        )

    def column_copy(step, d):
        return pltpu.make_async_remote_copy(
            src_ref=message.at[step, 0],
            dst_ref=column_in.at[step, d - 1],
            send_sem=column_send.at[step],
            recv_sem=column_recv.at[step],
            device_id=along(d),
            device_id_type=MESH,
        )

    def all_column(step):
        return pltpu.make_async_remote_copy(
            src_ref=column_in.at[step],
            dst_ref=column_in.at[step],
            send_sem=column_send.at[step],
            recv_sem=column_recv.at[step],
            device_id=along(1),
            device_id_type=MESH,
        )

    def plane_copy(step, d):
        return pltpu.make_async_remote_copy(
            src_ref=message.at[step, 1],
            dst_ref=plane_in.at[step, rank],
            send_sem=plane_send.at[step],
            recv_sem=plane_recv.at[step],
            device_id=across(d),
            device_id_type=MESH,
        )

    def all_plane(step):
        rows = plane_in.at[step, pl.ds(0, plane - 1)]
        return pltpu.make_async_remote_copy(
            src_ref=rows,
            dst_ref=rows,
            send_sem=plane_send.at[step],
            recv_sem=plane_recv.at[step],
            device_id=across(1),
            device_id_type=MESH,
        )

    for step in range(2):
        for j in range(6):

            @pl.when(jnp.logical_not(slots[j][2]))
            def _():
                ghost_in[step, j] = jnp.zeros((GHOST_TILES, 8, LANES), f32)

    zeros8 = jnp.zeros((8, LANES), f32)

    def squares(raw):
        return jnp.sum(jnp.where(sub < 3, raw * raw, 0.0), axis=0, keepdims=True)

    def source_rows(raw):
        mixed = jnp.where(sub < 3, raw, jnp.where(sub < 6, pltpu.roll(raw, 3, 0), 1.0))
        value = jnp.where(sub == 6, squares(raw), mixed)
        high, middle, low = split3(value)
        return [
            high,
            jnp.where(sub == 7, high, middle),
            jnp.where((sub < 3) | (sub == 6), low, high),
            zeros8,
        ]

    def target_rows(raw):
        mixed = jnp.where(sub < 3, -2.0 * raw, jnp.where(sub < 6, -2.0 * pltpu.roll(raw, 3, 0), 1.0))
        value = jnp.where(sub == 7, squares(raw) + core_sq, mixed)
        high, middle, low = split3(value)
        second = (sub >= 3) & (sub < 6)
        last = second | (sub == 7)
        return [
            jnp.where(second, middle, high),
            jnp.where(last, middle, high),
            jnp.where(last, low, high),
            zeros8,
        ]

    def strength_rows(raw):
        high = raw.astype(bf16).astype(f32)
        return jnp.concatenate([high, raw - high], axis=0).astype(bf16)

    def source_quad(quad, tiles):
        rows = [row for raw in tiles for row in source_rows(raw)]
        source_feat[quad] = jnp.transpose(jnp.concatenate(rows, axis=0)).astype(bf16)

    target_feat[...] = jnp.zeros_like(target_feat)

    chosen = (lax.broadcasted_iota(jnp.int32, (TILES, NPAIR), 0) == target_row[...].reshape(1, NPAIR))
    chosen = jnp.where(chosen, 1.0, 0.0).astype(bf16)
    chosen = jnp.concatenate([chosen, chosen], axis=1)

    pl.semaphore_wait(barrier, deep - 1 + plane - 1)

    velocity = None
    for step in range(2):

        def gather(g, c):
            index = ghost_list[pl.ds(pl.multiple_of(g * LANES, LANES), LANES)].reshape(1, LANES)
            low = jnp.broadcast_to(index & (LANES - 1), (8, LANES))
            high = jnp.broadcast_to(index >> 7, (8, LANES))
            found = zeros8
            for t in range(TILES):
                here = jnp.take_along_axis(
                    own[8 * t : 8 * t + 8, :], low, axis=1, mode="promise_in_bounds"
                )
                found = jnp.where(high == t, here, found)
            ghost_out[step, g] = found
            return c

        lax.fori_loop(0, GHOST_TILES, gather, 0)
        for j in range(6):

            @pl.when(slots[j][3])
            def _():
                ghost_copy(step, j).start()

        coords = [dense(k) for k in range(3)]
        centred = [coords[0], coords[1], coords[2] + ((gz.astype(f32) + 0.5) * side - 0.5)]
        powers = monomials(centred)
        for m, triple in enumerate(TRIPLES):
            for k in range(3):
                term = dense_strength[k]
                if powers[triple] is not None:
                    term = term * powers[triple]
                folded = functools.reduce(lambda a, b: a + b, [term[8 * i : 8 * i + 8] for i in range(TILES // 8)])
                partial[8 * (4 * m + k) : 8 * (4 * m + k) + 8, :] = folded
            if step == 0:
                partial[8 * (4 * m + 3) : 8 * (4 * m + 3) + 8, :] = zeros8
        summed = None
        for i in range(8):
            rows = partial[pl.ds(i, 4 * COUNT, stride=8), :]
            summed = rows if summed is None else summed + rows
        summed = jnp.concatenate([summed, jnp.zeros((MESSAGE - 4 * COUNT, LANES), f32)], axis=0)
        ones = jnp.ones((8, 3 * LANES), bf16)
        parts = jnp.concatenate([p.astype(bf16) for p in split3(summed)], axis=1)
        part = lax.dot_general(ones, parts, (((1,), (1,)), ((), ())), preferred_element_type=f32)[0:1]
        message[step, 0] = part

        def send_column(d, c):
            column_copy(step, d).start()
            return c

        lax.fori_loop(1, deep, send_column, 0)

        def own_quad(q, c):
            tiles = []
            for u in range(4):
                t = 4 * q + u
                raw = own[pl.ds(pl.multiple_of(8 * t, 8), 8), :]
                tiles.append(raw)
                rows = jnp.concatenate(target_rows(raw), axis=0).astype(bf16)
                for quarter in range(4):
                    target_feat[4 * t + quarter, 32 * quarter : 32 * quarter + 32, :] = rows
                if step == 0:
                    source_str[t] = strength_rows(raw)
            source_quad(q, tiles)
            return c

        lax.fori_loop(0, TILES // 4, own_quad, 0)

        if step == 0:
            separation = (
                away_x.astype(f32),
                away_y.astype(f32),
                jnp.full((4, plane), (gz.astype(f32) + 0.5) * side - 0.5, f32),
            )
            for q, value in enumerate(derivatives(separation).values()):
                far_weights[4 * q : 4 * q + 4, :] = value

        all_column(step).wait_recv()
        total = message[step, 0]
        for d in range(1, deep):
            total = total + column_in[step, d - 1]
        message[step, 1] = total
        plane_in[step, rank] = total

        def send_plane(d, c):
            plane_copy(step, d).start()
            return c

        lax.fori_loop(1, plane, send_plane, 0)

        for j in range(6):

            @pl.when(slots[j][2])
            def _():
                ghost_copy(step, j).wait_recv()

            axis, offset = slots[j][0], slots[j][1]
            moved = jnp.where(sub == axis, offset, 0.0)

            def ghost_quad(q, c):
                tiles = []
                for u in range(4):
                    raw = ghost_in[step, j, 4 * q + u]
                    tiles.append(raw + moved)
                    if step == 0:
                        source_str[TILES + j * GHOST_TILES + 4 * q + u] = strength_rows(raw)
                source_quad(TILES // 4 + j * (GHOST_TILES // 4) + q, tiles)
                return c

            lax.fori_loop(0, GHOST_TILES // 4, ghost_quad, 0)

        def near(b, c):
            values = []
            for u in range(UNROLL):
                p = b * UNROLL + u
                t, s = targets[p], sources[p]
                gap = jnp.dot(source_feat[s >> 2], target_feat[4 * t + (s & 3)], preferred_element_type=f32)
                values.append(halves(lax.rsqrt(jnp.maximum(gap, core_sq))))
            for u in range(UNROLL):
                p = b * UNROLL + u
                pushed = source_str[sources[p]]
                pushed = jnp.concatenate([pushed, pushed], axis=1)
                both = jnp.concatenate(values[u], axis=0)
                contrib[pl.ds(pl.multiple_of(16 * p, 16), 16), :] = jnp.dot(
                    pushed, both, preferred_element_type=f32
                )
            return c

        lax.fori_loop(0, NPAIR // UNROLL, near, 0)
        velocity = []
        for k in range(3):
            rows = contrib[pl.ds(3 + k, NPAIR, stride=16), :] + contrib[pl.ds(11 + k, NPAIR, stride=16), :]
            both = jnp.concatenate(halves(rows), axis=0)
            velocity.append(jnp.dot(chosen, both, preferred_element_type=f32))

        all_plane(step).wait_recv()
        for s in range(plane):
            gathered[s : s + 1, :] = plane_in[step, s]
        turned[...] = jnp.transpose(gathered[...])
        expansion = {}
        for m, inner in enumerate(TRIPLES):
            factor = (-1.0) ** sum(inner) / factorial(inner)
            source = jnp.where(is_far, turned[4 * m : 4 * m + 4, :] * factor, 0.0)
            for outer in TRIPLES:
                if sum(outer) + sum(inner) <= ORDER:
                    q = PLACE[tuple(a + b for a, b in zip(outer, inner))]
                    term = far_weights[4 * q : 4 * q + 4, :] * source
                    expansion[outer] = term if outer not in expansion else expansion[outer] + term
        for n, outer in enumerate(TRIPLES):
            value = jnp.sum(expansion[outer], axis=1, keepdims=True) * (1.0 / factorial(outer))
            local[4 * n : 4 * n + 4, :] = jnp.broadcast_to(value, (4, LANES))
        powers = monomials(coords)
        for n, outer in enumerate(TRIPLES):
            for k in range(3):
                term = jnp.broadcast_to(local[4 * n + k : 4 * n + k + 1, :], (TILES, LANES))
                if powers[outer] is not None:
                    term = term * powers[outer]
                velocity[k] = velocity[k] + term

        if step == 0:
            centre = (gx.astype(f32) + 0.5, gy.astype(f32) + 0.5, (gz.astype(f32) + 0.5) * side)
            block_out[...] = jnp.zeros_like(block_out)
            for k in range(3):
                moved = coords[k] + time_step * velocity[k]
                own[pl.ds(k, TILES, stride=8), :] = moved
                place(0, k, moved + centre[k])
            send_blocks(0)

    for k in range(3):
        place(1, k, velocity[k])
    send_blocks(1)
    all_blocks(0).wait_recv()
    all_blocks(1).wait_recv()
    for s in range(plane):
        start = block_in[8 * s : 8 * s + 8, :]
        speed = block_in[8 * (plane + s) : 8 * (plane + s) + 8, :]
        ended = start + time_step * speed
        for r in range(CAP):
            out_pos[CAP * s + r] = ended[3 * r : 3 * r + 3]
            out_vel[CAP * s + r] = speed[3 * r : 3 * r + 3]

    for step in range(2):
        for j in range(6):

            @pl.when(slots[j][3])
            def _():
                ghost_copy(step, j).wait_send()

        all_column(step).wait_send()
        all_plane(step).wait_send()
        all_blocks(step).wait_send()


def per_device(offsets, strength, ghost_list, pair_targets, pair_sources, owners):
    sizes = tuple(lax.axis_size(axis) for axis in ("gx", "gy", "gz"))
    wide, tall, deep = sizes
    plane = wide * tall
    vmem = pl.BlockSpec(memory_space=pltpu.VMEM)
    smem = pl.BlockSpec(memory_space=pltpu.SMEM)
    shape = jax.ShapeDtypeStruct((plane * CAP, 3, LANES), f32)
    dma = pltpu.SemaphoreType.DMA
    return pl.pallas_call(
        functools.partial(kernel, sizes),
        out_shape=(shape, shape),
        in_specs=[vmem, vmem, vmem, smem, vmem, smem, vmem],
        out_specs=(vmem, vmem),
        scratch_shapes=[
            pltpu.VMEM((8 * TILES, LANES), f32),
            pltpu.VMEM((2, GHOST_TILES, 8, LANES), f32),
            pltpu.VMEM((2, 6, GHOST_TILES, 8, LANES), f32),
            pltpu.VMEM((4 * TILES, LANES, LANES), bf16),
            pltpu.VMEM((SOURCES // 4, LANES, LANES), bf16),
            pltpu.VMEM((SOURCES, 16, LANES), bf16),
            pltpu.VMEM((NPAIR * 16, LANES), f32),
            pltpu.VMEM((4 * COUNT * 8, LANES), f32),
            pltpu.VMEM((2, 2, 1, MESSAGE), f32),
            pltpu.VMEM((2, deep - 1, 1, MESSAGE), f32),
            pltpu.VMEM((2, plane, 1, MESSAGE), f32),
            pltpu.VMEM((plane, MESSAGE), f32),
            pltpu.VMEM((MESSAGE, plane), f32),
            pltpu.VMEM((4 * COUNT, LANES), f32),
            pltpu.VMEM((4 * COUNT, plane), f32),
            pltpu.VMEM((2 * plane * 8, LANES), f32),
            pltpu.VMEM((2 * plane * 8, LANES), f32),
            dma((2, 6)),
            dma((2, 6)),
            dma((2,)),
            dma((2,)),
            dma((2,)),
            dma((2,)),
            dma((2,)),
            dma((2,)),
        ],
        compiler_params=pltpu.CompilerParams(
            collective_id=0, has_side_effects=True, vmem_limit_bytes=40 << 20
        ),
        name="dislocation_steps",
    )(offsets, strength, ghost_list, pair_targets, pair_targets, pair_sources, owners)


def solution(mesh):
    return jax.shard_map(
        per_device,
        mesh=mesh,
        in_specs=(
            P(None, ("gx", "gy", "gz")),
            P(None, ("gx", "gy", "gz")),
            P(("gx", "gy", "gz")),
            P(("gx", "gy", "gz")),
            P(("gx", "gy", "gz")),
            P(("gx", "gy", "gz"), None),
        ),
        out_specs=(P(("gx", "gy", "gz"), None, None), P(("gx", "gy", "gz"), None, None)),
        check_vma=False,
    )
```

profile of v0, /device:TPU:1, one launch (start us, length us, event | category | flops | bytes accessed | tf_op | source)
XLA Modules:
  0.0 47.7 jit_solution(6484177280218514728)
XLA Ops:
  0.6 0.0 copy-start.4
  0.6 0.0 copy-start.3
  0.7 0.0 copy-start.2
  0.7 0.8 %copy.8.owners = s32[32,1]{1,0:T(8,128)S(1)} copy(s32[32,1]{0,1:T(1,128)} %param.11) | data formatting | bytes 256 | tf_op args[5]
  1.4 0.0 copy-done.4
  1.4 0.0 copy-done.3
  1.4 0.0 copy-done.2
  1.4 0.0 copy-start
  1.4 0.8 %copy-done = f32[3,4096]{1,0:T(4,128)S(1)} copy-done((f32[3,4096]{1,0:T(4,128)S(1)}, f32[3,4096]{1,0:T(4,128)}, u32[]{:S(2)}) %copy-start) | copy-done | bytes 49176
  2.3 0.0 copy-start.1
  2.3 0.8 %copy-done.1 = f32[3,4096]{1,0:T(4,128)S(1)} copy-done((f32[3,4096]{1,0:T(4,128)S(1)}, f32[3,4096]{1,0:T(4,128)}, u32[]{:S(2)}) %copy-start.1) | copy-done | bytes 49176
  3.1 43.3 %dislocation_steps.1 = (f32[64,3,128]{2,1,0:T(4,128)S(1)}, f32[64,3,128]{2,1,0:T(4,128)S(1)}) custom-call(f32[3,4096]{1,0:T(4,128)S(1)} %copy-done, f32[3,4096]{1,0:T(4,128)S(1)} %copy-done.1, s32[1536]{0:T(1024)S(1)} %copy-done.2, s32[128]{0:T(128)S(1)} %copy-done.3, s32[128]{0:T(128)S(1)} %copy-done.3, s32[128]{0:T(128)S(1)} %copy-done.4, ...), custom_call_target="tpu_custom_call" | custom-call | tf_op jit(solution)/shard_map/dislocation_steps/pallas_call | solution.py:513
  46.4 0.6 %copy.9 = f32[64,3,128]{2,0,1:T(8,128)} copy(f32[64,3,128]{2,1,0:T(4,128)S(1)} %get-tuple-element.2) | data formatting | bytes 196608 | tf_op jit(solution)/shard_map/dislocation_steps/pallas_call | solution.py:513
  47.1 0.6 %copy.10 = f32[64,3,128]{2,0,1:T(8,128)} copy(f32[64,3,128]{2,1,0:T(4,128)S(1)} %get-tuple-element.3) | data formatting | bytes 196608 | tf_op jit(solution)/shard_map/dislocation_steps/pallas_call | solution.py:513
Async XLA Ops:
  0.6 0.8 %copy-start.4 = (s32[128]{0:T(128)S(1)}, s32[128]{0:T(128)}, u32[]{:S(2)}) copy-start(s32[128]{0:T(128)} %sources.1) | copy-start | bytes 1540
  0.6 0.8 %copy-start.3 = (s32[128]{0:T(128)S(1)}, s32[128]{0:T(128)}, u32[]{:S(2)}) copy-start(s32[128]{0:T(128)} %target_row.1) | copy-start | bytes 1540
  0.7 0.8 %copy-start.2 = (s32[1536]{0:T(1024)S(1)}, s32[1536]{0:T(1024)}, u32[]{:S(2)}) copy-start(s32[1536]{0:T(1024)} %ghost_list.1) | copy-start | bytes 18436
  1.4 0.8 %copy-start = (f32[3,4096]{1,0:T(4,128)S(1)}, f32[3,4096]{1,0:T(4,128)}, u32[]{:S(2)}) copy-start(f32[3,4096]{1,0:T(4,128)} %offsets.1) | copy-start | bytes 147460
  2.3 0.8 %copy-start.1 = (f32[3,4096]{1,0:T(4,128)S(1)}, f32[3,4096]{1,0:T(4,128)}, u32[]{:S(2)}) copy-start(f32[3,4096]{1,0:T(4,128)} %strength.1) | copy-start | bytes 147460
where the time goes:
time: 48 us; the launch traced here: 47.7 us
  Pallas kernels  43.3 us (90%)
  local copies, waits for them, and re-layouts  3.73 us (8%)
  between operations  0.68 us (1%)
    pallas_call x1, Pallas kernels, per_device(): pl.pallas_call(functools.partial(kernel, sizes), out_shape=(shape, shape)...  43.3 us
    unnamed x11, local copies, waits for them, and re-layouts  2.44 us
    pallas_call x2, local copies, waits for them, and re-layouts, per_device(): pl.pallas_call(functools.partial(kernel, sizes), out_shape=(shape, shape)...  1.29 us

commit v1 on v0

--- a/solution.py
+++ b/solution.py
@@ -18,7 +18,7 @@
 TILES = SEG // LANES
 GHOST_TILES = GHOST // LANES
 SOURCES = TILES + 6 * GHOST_TILES
-UNROLL = 16
+UNROLL = 32
 
 core_sq = 0.0025
 time_step = 0.1
@@ -94,9 +94,10 @@
 
 def kernel(
     sizes,
-    offsets, strength, ghost_list, targets, target_row, sources, owners,
-    out_pos, out_vel,
-    own, ghost_out, ghost_in, target_feat, source_feat, source_str, contrib, partial,
+    offsets_in, strength_in, ghost_list, targets, target_row, sources, owners,
+    out_start, out_speed,
+    offsets, strength, input_done,
+    own, paired, ghost_out, ghost_in, ghost_out_late, ghost_in_late, target_feat, source_feat, source_str, contrib, partial,
     message, column_in, plane_in, gathered, turned, local, far_weights, block_out, block_in,
     ghost_send, ghost_recv, column_send, column_recv, plane_send, plane_recv, block_send, block_recv,
 ):
@@ -104,15 +105,21 @@
     plane = wide * tall
     gx, gy, gz = lax.axis_index("gx"), lax.axis_index("gy"), lax.axis_index("gz")
     rank = gx * tall + gy
+    shift = tall.bit_length() - 1
     side = 1.0 / deep
     sub = lax.broadcasted_iota(jnp.int32, (8, LANES), 0)
 
     def along(d):
-        return (gx, gy, lax.rem(gz + d, deep))
+        return (gx, gy, (gz + d) & (deep - 1))
 
     def across(d):
-        other = lax.rem(rank + d, plane)
-        return (other // tall, lax.rem(other, tall), gz)
+        other = (rank + d) & (plane - 1)
+        return (other >> shift, other & (tall - 1), gz)
+
+    load_offsets = pltpu.make_async_copy(offsets_in, offsets, input_done.at[0])
+    load_strength = pltpu.make_async_copy(strength_in, strength, input_done.at[1])
+    load_offsets.start()
+    load_strength.start()
 
     barrier = pltpu.get_barrier_semaphore()
 
@@ -139,6 +146,10 @@
 
     scale = jnp.where(lax.broadcasted_iota(jnp.int32, (3, LANES), 0) == 2, side, 1.0)
     own[...] = jnp.zeros_like(own)
+    target_feat[...] = jnp.zeros_like(target_feat)
+    block_out[...] = jnp.zeros_like(block_out)
+    load_offsets.wait()
+    load_strength.wait()
     for t in range(TILES):
         lanes = slice(t * LANES, (t + 1) * LANES)
         own[8 * t : 8 * t + 3, :] = (offsets[:, lanes] - 0.5) * scale
@@ -150,16 +161,14 @@
     dense_strength = [dense(3 + k) for k in range(3)]
 
     lane = lax.broadcasted_iota(jnp.int32, (4, plane), 1)
-    shift = tall.bit_length() - 1
     source_x, source_y = lane >> shift, lane & (tall - 1)
     away_x, away_y = gx - source_x, gy - source_y
     is_far = jnp.maximum(jnp.abs(away_x), jnp.abs(away_y)) >= 3
 
-    column = owners[...]
     rows_i = lax.broadcasted_iota(jnp.int32, (TILES, TILES), 0)
     cols_i = lax.broadcasted_iota(jnp.int32, (TILES, TILES), 1)
-    column_f = jnp.broadcast_to(column.astype(f32), (TILES, TILES))
-    row_f = jnp.sum(jnp.where(rows_i == cols_i, column_f, 0.0), axis=0, keepdims=True)
+    row_f = owners[...].astype(f32)
+    column_f = jnp.sum(jnp.where(rows_i == cols_i, row_f, 0.0), axis=1, keepdims=True)
     earlier = jnp.where((column_f == row_f) & (rows_i < cols_i), 1.0, 0.0)
     slot_f = jnp.sum(earlier, axis=0, keepdims=True) * plane + row_f
     slot_rows = lax.broadcasted_iota(jnp.int32, (CAP * plane, TILES), 0).astype(f32)
@@ -209,8 +218,8 @@
 
     def ghost_copy(step, j):
         return pltpu.make_async_remote_copy(
-            src_ref=ghost_out.at[step],
-            dst_ref=ghost_in.at[step, j],
+            src_ref=ghost_out if step == 0 else ghost_out_late,
+            dst_ref=ghost_in.at[j] if step == 0 else ghost_in_late.at[j],
             send_sem=ghost_send.at[step, j],
             recv_sem=ghost_recv.at[step, j],
             device_id=slots[j][4],
@@ -258,13 +267,14 @@
             device_id_type=MESH,
         )
 
-    for step in range(2):
-        for j in range(6):
-
-            @pl.when(jnp.logical_not(slots[j][2]))
-            def _():
-                ghost_in[step, j] = jnp.zeros((GHOST_TILES, 8, LANES), f32)
-
+    for j in range(6):
+
+        @pl.when(jnp.logical_not(slots[j][2]))
+        def _():
+            ghost_in[j] = jnp.zeros((GHOST_TILES, 8, LANES), f32)
+            ghost_in_late[j] = jnp.zeros((GHOST_TILES // 2, 8, LANES), f32)
+
+    centre = (gx.astype(f32) + 0.5, gy.astype(f32) + 0.5, (gz.astype(f32) + 0.5) * side)
     zeros8 = jnp.zeros((8, LANES), f32)
 
     def squares(raw):
@@ -302,36 +312,59 @@
         rows = [row for raw in tiles for row in source_rows(raw)]
         source_feat[quad] = jnp.transpose(jnp.concatenate(rows, axis=0)).astype(bf16)
 
-    target_feat[...] = jnp.zeros_like(target_feat)
-
     chosen = (lax.broadcasted_iota(jnp.int32, (TILES, NPAIR), 0) == target_row[...].reshape(1, NPAIR))
     chosen = jnp.where(chosen, 1.0, 0.0).astype(bf16)
     chosen = jnp.concatenate([chosen, chosen], axis=1)
 
-    pl.semaphore_wait(barrier, deep - 1 + plane - 1)
-
-    velocity = None
-    for step in range(2):
-
-        def gather(g, c):
-            index = ghost_list[pl.ds(pl.multiple_of(g * LANES, LANES), LANES)].reshape(1, LANES)
-            low = jnp.broadcast_to(index & (LANES - 1), (8, LANES))
-            high = jnp.broadcast_to(index >> 7, (8, LANES))
+    def ghost_index(g):
+        index = ghost_list[pl.ds(pl.multiple_of(g * LANES, LANES), LANES)].reshape(1, LANES)
+        return jnp.broadcast_to(index & (LANES - 1), (8, LANES)), jnp.broadcast_to(index >> 7, (8, LANES))
+
+    def take(tile, low):
+        return jnp.take_along_axis(tile, low, axis=1, mode="promise_in_bounds")
+
+    def gather_all(step):
+        def whole(g, c):
+            low, high = ghost_index(g)
             found = zeros8
             for t in range(TILES):
-                here = jnp.take_along_axis(
-                    own[8 * t : 8 * t + 8, :], low, axis=1, mode="promise_in_bounds"
-                )
-                found = jnp.where(high == t, here, found)
-            ghost_out[step, g] = found
+                found = jnp.where(high == t, take(own[8 * t : 8 * t + 8, :], low), found)
+            ghost_out[g] = found
             return c
 
-        lax.fori_loop(0, GHOST_TILES, gather, 0)
+        def pair(g, c):
+            both = []
+            for u in range(2):
+                low, high = ghost_index(2 * g + u)
+                high = high - (sub >> 2)
+                found = zeros8
+                for t in range(TILES // 2):
+                    found = jnp.where(high == 2 * t, take(paired[t], low), found)
+                both.append(found + pltpu.roll(found, 4, 0))
+            ghost_out_late[g] = jnp.where(sub < 4, both[0], both[1])
+            return c
+
+        if step == 0:
+            lax.fori_loop(0, GHOST_TILES, whole, 0)
+        else:
+            for t in range(TILES // 2):
+                first, second = own[16 * t : 16 * t + 8, :], own[16 * t + 8 : 16 * t + 16, :]
+                paired[t] = jnp.where(sub < 4, first, pltpu.roll(second, 4, 0))
+            lax.fori_loop(0, GHOST_TILES // 2, pair, 0)
+
+    def send_ghosts(step):
         for j in range(6):
 
             @pl.when(slots[j][3])
             def _():
                 ghost_copy(step, j).start()
+
+    velocity = None
+    for step in range(2):
+
+        gather_all(step)
+        if step == 1:
+            send_ghosts(step)
 
         coords = [dense(k) for k in range(3)]
         centred = [coords[0], coords[1], coords[2] + ((gz.astype(f32) + 0.5) * side - 0.5)]
@@ -359,9 +392,15 @@
             column_copy(step, d).start()
             return c
 
-        lax.fori_loop(1, deep, send_column, 0)
-
-        def own_quad(q, c):
+        if step == 1:
+            lax.fori_loop(1, deep, send_column, 0)
+
+        def own_quads(i, c):
+            for v in range(4):
+                own_quad(4 * i + v)
+            return c
+
+        def own_quad(q):
             tiles = []
             for u in range(4):
                 t = 4 * q + u
@@ -373,9 +412,8 @@
                 if step == 0:
                     source_str[t] = strength_rows(raw)
             source_quad(q, tiles)
-            return c
-
-        lax.fori_loop(0, TILES // 4, own_quad, 0)
+
+        lax.fori_loop(0, TILES // 16, own_quads, 0)
 
         if step == 0:
             separation = (
@@ -386,6 +424,14 @@
             for q, value in enumerate(derivatives(separation).values()):
                 far_weights[4 * q : 4 * q + 4, :] = value
 
+            pl.semaphore_wait(barrier, deep - 1 + plane - 1)
+            send_ghosts(step)
+            lax.fori_loop(1, deep, send_column, 0)
+        else:
+            for k in range(3):
+                place(0, k, coords[k] + centre[k])
+            send_blocks(0)
+
         all_column(step).wait_recv()
         total = message[step, 0]
         for d in range(1, deep):
@@ -408,17 +454,19 @@
             axis, offset = slots[j][0], slots[j][1]
             moved = jnp.where(sub == axis, offset, 0.0)
 
-            def ghost_quad(q, c):
+            for q in range(GHOST_TILES // 4):
                 tiles = []
                 for u in range(4):
-                    raw = ghost_in[step, j, 4 * q + u]
+                    g = 4 * q + u
+                    if step == 0:
+                        raw = ghost_in[j, g]
+                        source_str[TILES + j * GHOST_TILES + g] = strength_rows(raw)
+                    elif u % 2 == 0:
+                        raw = ghost_in_late[j, g // 2]
+                    else:
+                        raw = pltpu.roll(ghost_in_late[j, g // 2], 4, 0)
                     tiles.append(raw + moved)
-                    if step == 0:
-                        source_str[TILES + j * GHOST_TILES + 4 * q + u] = strength_rows(raw)
                 source_quad(TILES // 4 + j * (GHOST_TILES // 4) + q, tiles)
-                return c
-
-            lax.fori_loop(0, GHOST_TILES // 4, ghost_quad, 0)
 
         def near(b, c):
             values = []
@@ -469,26 +517,19 @@
                 velocity[k] = velocity[k] + term
 
         if step == 0:
-            centre = (gx.astype(f32) + 0.5, gy.astype(f32) + 0.5, (gz.astype(f32) + 0.5) * side)
-            block_out[...] = jnp.zeros_like(block_out)
             for k in range(3):
-                moved = coords[k] + time_step * velocity[k]
-                own[pl.ds(k, TILES, stride=8), :] = moved
-                place(0, k, moved + centre[k])
-            send_blocks(0)
+                own[pl.ds(k, TILES, stride=8), :] = coords[k] + time_step * velocity[k]
 
     for k in range(3):
         place(1, k, velocity[k])
     send_blocks(1)
     all_blocks(0).wait_recv()
     all_blocks(1).wait_recv()
-    for s in range(plane):
-        start = block_in[8 * s : 8 * s + 8, :]
-        speed = block_in[8 * (plane + s) : 8 * (plane + s) + 8, :]
-        ended = start + time_step * speed
-        for r in range(CAP):
-            out_pos[CAP * s + r] = ended[3 * r : 3 * r + 3]
-            out_vel[CAP * s + r] = speed[3 * r : 3 * r + 3]
+    for which, out in ((0, out_start), (1, out_speed)):
+        for k in range(3):
+            for r in range(CAP):
+                rows = pl.ds(which * plane * 8 + 3 * r + k, plane, stride=8)
+                out[k, pl.ds(r, plane, stride=CAP), :] = block_in[rows, :]
 
     for step in range(2):
         for j in range(6):
@@ -500,6 +541,11 @@
         all_column(step).wait_send()
         all_plane(step).wait_send()
         all_blocks(step).wait_send()
+
+
+def finish(start, speed):
+    moved = start + time_step * speed
+    return moved.transpose(1, 0, 2), speed.transpose(1, 0, 2)
 
 
 def per_device(offsets, strength, ghost_list, pair_targets, pair_sources, owners):
@@ -508,17 +554,24 @@
     plane = wide * tall
     vmem = pl.BlockSpec(memory_space=pltpu.VMEM)
     smem = pl.BlockSpec(memory_space=pltpu.SMEM)
-    shape = jax.ShapeDtypeStruct((plane * CAP, 3, LANES), f32)
+    hbm = pl.BlockSpec(memory_space=pltpu.HBM)
+    shape = jax.ShapeDtypeStruct((3, plane * CAP, LANES), f32)
     dma = pltpu.SemaphoreType.DMA
-    return pl.pallas_call(
+    start, speed = pl.pallas_call(
         functools.partial(kernel, sizes),
         out_shape=(shape, shape),
-        in_specs=[vmem, vmem, vmem, smem, vmem, smem, vmem],
+        in_specs=[hbm, hbm, vmem, smem, vmem, smem, vmem],
         out_specs=(vmem, vmem),
         scratch_shapes=[
+            pltpu.VMEM((3, SEG), f32),
+            pltpu.VMEM((3, SEG), f32),
+            pltpu.SemaphoreType.DMA((2,)),
             pltpu.VMEM((8 * TILES, LANES), f32),
-            pltpu.VMEM((2, GHOST_TILES, 8, LANES), f32),
-            pltpu.VMEM((2, 6, GHOST_TILES, 8, LANES), f32),
+            pltpu.VMEM((TILES // 2, 8, LANES), f32),
+            pltpu.VMEM((GHOST_TILES, 8, LANES), f32),
+            pltpu.VMEM((6, GHOST_TILES, 8, LANES), f32),
+            pltpu.VMEM((GHOST_TILES // 2, 8, LANES), f32),
+            pltpu.VMEM((6, GHOST_TILES // 2, 8, LANES), f32),
             pltpu.VMEM((4 * TILES, LANES, LANES), bf16),
             pltpu.VMEM((SOURCES // 4, LANES, LANES), bf16),
             pltpu.VMEM((SOURCES, 16, LANES), bf16),
@@ -543,10 +596,11 @@
             dma((2,)),
         ],
         compiler_params=pltpu.CompilerParams(
-            collective_id=0, has_side_effects=True, vmem_limit_bytes=40 << 20
+            collective_id=0, has_side_effects=True, vmem_limit_bytes=62 << 20
         ),
         name="dislocation_steps",
-    )(offsets, strength, ghost_list, pair_targets, pair_targets, pair_sources, owners)
+    )(offsets, strength, ghost_list, pair_targets, pair_targets, pair_sources, owners.reshape(1, TILES))
+    return finish(start, speed)
 
 
 def solution(mesh):

time: 48 us -> 42.4 us (0.88)
  Pallas kernels: 43.3 us -> 39.1 us
  local copies, waits for them, and re-layouts: 3.73 us -> 0.64 us
  other arithmetic: 0 us -> 1.63 us
    pallas_call x1, Pallas kernels: 43.3 us -> 39.1 us  [per_device(): pl.pallas_call(functools.partial(kernel, sizes), out_shape=(shape, shape)...]
    unnamed x11 -> x3, local copies, waits for them, and re-layouts: 2.44 us -> 0.64 us
    transpose x0 -> x1, other arithmetic: none -> 1.63 us  [finish(): return (moved.transpose(1, 0, 2), speed.transpose(1, 0, 2))]
    pallas_call x2 -> x0, local copies, waits for them, and re-layouts: 1.29 us -> none  [per_device(): pl.pallas_call(functools.partial(kernel, sizes), out_shape=(shape, shape)...]
where the time goes in v1:
time: 42.4 us; the launch traced here: 42 us
  Pallas kernels  39.1 us (92%)
  other arithmetic  1.63 us (4%)
  between operations  0.65 us (2%)
  local copies, waits for them, and re-layouts  0.64 us (2%)
    pallas_call x1, Pallas kernels, per_device(): pl.pallas_call(functools.partial(kernel, sizes), out_shape=(shape, shape)...  39.1 us
    transpose x1, other arithmetic, finish(): return (moved.transpose(1, 0, 2), speed.transpose(1, 0, 2))  1.63 us

profile of v1, /device:TPU:1, one launch (start us, length us, event | category | flops | bytes accessed | tf_op | source)
XLA Modules:
  0.0 42.0 jit_solution(9514667085016246681)
XLA Ops:
  0.6 39.1 %dislocation_steps.1 = (f32[3,64,128]{2,1,0:T(8,128)}, f32[3,64,128]{2,1,0:T(8,128)}) custom-call(f32[3,4096]{1,0:T(4,128)} %offsets_in.1, f32[3,4096]{1,0:T(4,128)} %strength_in.1, s32[1536]{0:T(1024)} %ghost_list.1, s32[128]{0:T(128)} %target_row.1, s32[128]{0:T(128)} %target_row.1, s32[128]{0:T(128)} %sources.1, s32[1,32]{1,0:T(1,128)} %bitcast.5), custom_call_target="tpu_custom_call" | custom-call | tf_op jit(solution)/shard_map/dislocation_steps/pallas_call | solution.py:560
  39.7 0.0 copy-start
  39.7 1.6 %add_bitcast_fusion = f32[64,3,128]{2,0,1:T(8,128)} fusion(f32[3,64,128]{2,1,0:T(8,128)} %get-tuple-element.4, f32[3,64,128]{2,1,0:T(8,128)} %get-tuple-element.5), kind=kLoop, calls=%fused_computation | loop fusion | flops 49152 | bytes 294912 | tf_op jit(solution)/shard_map/transpose | solution.py:548
  41.3 0.0 copy-done
  41.3 0.6 %copy.9 = f32[64,3,128]{2,0,1:T(8,128)} copy(f32[64,3,128]{2,0,1:T(8,128)S(1)} %bitcast.4) | data formatting | bytes 196608
Async XLA Ops:
  39.7 1.6 %copy-start = (f32[3,64,128]{2,1,0:T(8,128)S(1)}, f32[3,64,128]{2,1,0:T(8,128)}, u32[]{:S(2)}) copy-start(f32[3,64,128]{2,1,0:T(8,128)} %get-tuple-element.5) | copy-start | bytes 294916

commit v2 on v1

--- a/solution.py
+++ b/solution.py
@@ -98,7 +98,8 @@
     out_start, out_speed,
     offsets, strength, input_done,
     own, paired, ghost_out, ghost_in, ghost_out_late, ghost_in_late, target_feat, source_feat, source_str, contrib, partial,
-    message, column_in, plane_in, gathered, turned, local, far_weights, block_out, block_in,
+    message, column_in, plane_in, gathered, turned, local, far_weights,
+    start_flat, start_out, start_mid, start_in, speed_out, speed_in,
     ghost_send, ghost_recv, column_send, column_recv, plane_send, plane_recv, block_send, block_recv,
 ):
     wide, tall, deep = sizes
@@ -113,26 +114,30 @@
         return (gx, gy, (gz + d) & (deep - 1))
 
     def across(d):
-        other = (rank + d) & (plane - 1)
-        return (other >> shift, other & (tall - 1), gz)
+        return ((gx + d[0]) & (wide - 1), (gy + d[1]) & (tall - 1), gz)
+
+    def hops(d):
+        return min(d[0], wide - d[0]) + min(d[1], tall - d[1])
+
+    others = [(x, y) for x in range(wide) for y in range(tall) if x + y > 0]
+    others.sort(key=hops, reverse=True)
 
     load_offsets = pltpu.make_async_copy(offsets_in, offsets, input_done.at[0])
     load_strength = pltpu.make_async_copy(strength_in, strength, input_done.at[1])
     load_offsets.start()
     load_strength.start()
 
+    def along_y(d):
+        return (gx, (gy + d) & (tall - 1), gz)
+
+    def along_x(d):
+        return ((gx + d) & (wide - 1), gy, gz)
+
     barrier = pltpu.get_barrier_semaphore()
 
-    def greet_column(d, c):
-        pl.semaphore_signal(barrier, inc=1, device_id=along(d), device_id_type=MESH)
-        return c
-
-    def greet_plane(d, c):
-        pl.semaphore_signal(barrier, inc=1, device_id=across(d), device_id_type=MESH)
-        return c
-
-    lax.fori_loop(1, deep, greet_column, 0)
-    lax.fori_loop(1, plane, greet_plane, 0)
+    partners = [across(d) for d in others] + [along(d) for d in range(1, deep)]
+    for partner in partners:
+        pl.semaphore_signal(barrier, inc=1, device_id=partner, device_id_type=MESH)
 
     position = (gx, gy, gz)
     slots = []
@@ -147,7 +152,8 @@
     scale = jnp.where(lax.broadcasted_iota(jnp.int32, (3, LANES), 0) == 2, side, 1.0)
     own[...] = jnp.zeros_like(own)
     target_feat[...] = jnp.zeros_like(target_feat)
-    block_out[...] = jnp.zeros_like(block_out)
+    start_flat[...] = jnp.zeros_like(start_flat)
+    speed_out[...] = jnp.zeros_like(speed_out)
     load_offsets.wait()
     load_strength.wait()
     for t in range(TILES):
@@ -170,51 +176,66 @@
     row_f = owners[...].astype(f32)
     column_f = jnp.sum(jnp.where(rows_i == cols_i, row_f, 0.0), axis=1, keepdims=True)
     earlier = jnp.where((column_f == row_f) & (rows_i < cols_i), 1.0, 0.0)
-    slot_f = jnp.sum(earlier, axis=0, keepdims=True) * plane + row_f
+    nth_f = jnp.sum(earlier, axis=0, keepdims=True) * plane
     slot_rows = lax.broadcasted_iota(jnp.int32, (CAP * plane, TILES), 0).astype(f32)
-    placer = jnp.where(slot_rows == slot_f, 1.0, 0.0).astype(bf16)
-    placer = jnp.concatenate([placer, placer, placer], axis=1)
-
-    def place(which, k, field):
+
+    def placer_of(order_f):
+        placer = jnp.where(slot_rows == nth_f + order_f, 1.0, 0.0).astype(bf16)
+        return jnp.concatenate([placer, placer, placer], axis=1)
+
+    row_i = owners[...]
+    placer_start = placer_of(((row_i & (tall - 1)) * wide + (row_i >> shift)).astype(f32))
+    placer_speed = placer_of(row_f)
+
+    def place(placer, out, k, field):
         parts = jnp.concatenate([p.astype(bf16) for p in split3(field)], axis=0)
         placed = jnp.dot(placer, parts, preferred_element_type=f32)
         for r in range(CAP):
-            rows = pl.ds(which * plane * 8 + 3 * r + k, plane, stride=8)
-            block_out[rows, :] = placed[r * plane : (r + 1) * plane]
-
-    def block_rows(which, o):
-        return pl.ds(pl.multiple_of(which * plane * 8 + 8 * o, 8), 8)
-
-    def block_copy(which, d):
+            out[pl.ds(3 * r + k, plane, stride=8), :] = placed[r * plane : (r + 1) * plane]
+
+    def remote(src, dst, send_sem, recv_sem, device):
+        return pltpu.make_async_remote_copy(
+            src_ref=src,
+            dst_ref=dst,
+            send_sem=send_sem,
+            recv_sem=recv_sem,
+            device_id=device,
+            device_id_type=MESH,
+        )
+
+    def speed_rows(o):
+        return pl.ds(pl.multiple_of(8 * o, 8), 3 * CAP)
+
+    def speed_copy(d):
         target = across(d)
         other = target[0] * tall + target[1]
-        return pltpu.make_async_remote_copy(
-            src_ref=block_out.at[block_rows(which, other)],
-            dst_ref=block_in.at[block_rows(which, rank)],
-            send_sem=block_send.at[which],
-            recv_sem=block_recv.at[which],
-            device_id=target,
-            device_id_type=MESH,
-        )
-
-    def send_blocks(which):
-        def send(d, c):
-            block_copy(which, d).start()
-            return c
-
-        lax.fori_loop(1, plane, send, 0)
-        block_in[block_rows(which, rank), :] = block_out[block_rows(which, rank), :]
-
-    def all_blocks(which):
-        rows = pl.ds(which * plane * 8, (plane - 1) * 8)
-        return pltpu.make_async_remote_copy(
-            src_ref=block_out.at[rows],
-            dst_ref=block_in.at[rows],
-            send_sem=block_send.at[which],
-            recv_sem=block_recv.at[which],
-            device_id=across(1),
-            device_id_type=MESH,
-        )
+        return remote(
+            speed_out.at[speed_rows(other)], speed_in.at[speed_rows(rank)], block_send.at[0], block_recv.at[0], target
+        )
+
+    def all_speed():
+        rows = pl.ds(0, (plane - 1) * 3 * CAP)
+        return remote(speed_out.at[rows], speed_in.at[rows], block_send.at[0], block_recv.at[0], across(others[0]))
+
+    def start_y_copy(d):
+        target = along_y(d)
+        return remote(
+            start_out.at[target[1]], start_mid.at[:, gy], block_send.at[1], block_recv.at[1], target
+        )
+
+    def all_start_y():
+        part = start_mid.at[:, pl.ds(0, tall - 1)]
+        return remote(part, part, block_send.at[1], block_recv.at[1], along_y(1))
+
+    def start_x_copy(d):
+        target = along_x(d)
+        return remote(
+            start_mid.at[target[0]], start_in.at[gx], block_send.at[2], block_recv.at[2], target
+        )
+
+    def all_start_x():
+        part = start_in.at[pl.ds(0, wide - 1)]
+        return remote(part, part, block_send.at[2], block_recv.at[2], along_x(1))
 
     def ghost_copy(step, j):
         return pltpu.make_async_remote_copy(
@@ -247,25 +268,13 @@
         )
 
     def plane_copy(step, d):
-        return pltpu.make_async_remote_copy(
-            src_ref=message.at[step, 1],
-            dst_ref=plane_in.at[step, rank],
-            send_sem=plane_send.at[step],
-            recv_sem=plane_recv.at[step],
-            device_id=across(d),
-            device_id_type=MESH,
+        return remote(
+            message.at[step, 1], plane_in.at[step, rank], plane_send.at[step], plane_recv.at[step], across(d)
         )
 
     def all_plane(step):
         rows = plane_in.at[step, pl.ds(0, plane - 1)]
-        return pltpu.make_async_remote_copy(
-            src_ref=rows,
-            dst_ref=rows,
-            send_sem=plane_send.at[step],
-            recv_sem=plane_recv.at[step],
-            device_id=across(1),
-            device_id_type=MESH,
-        )
+        return remote(rows, rows, plane_send.at[step], plane_recv.at[step], across(others[0]))
 
     for j in range(6):
 
@@ -361,10 +370,6 @@
 
     velocity = None
     for step in range(2):
-
-        gather_all(step)
-        if step == 1:
-            send_ghosts(step)
 
         coords = [dense(k) for k in range(3)]
         centred = [coords[0], coords[1], coords[2] + ((gz.astype(f32) + 0.5) * side - 0.5)]
@@ -388,12 +393,14 @@
         part = lax.dot_general(ones, parts, (((1,), (1,)), ((), ())), preferred_element_type=f32)[0:1]
         message[step, 0] = part
 
-        def send_column(d, c):
+        if step == 0:
+            gather_all(step)
+            pl.semaphore_wait(barrier, len(partners))
+        for d in range(1, deep):
             column_copy(step, d).start()
-            return c
-
         if step == 1:
-            lax.fori_loop(1, deep, send_column, 0)
+            gather_all(step)
+        send_ghosts(step)
 
         def own_quads(i, c):
             for v in range(4):
@@ -424,13 +431,16 @@
             for q, value in enumerate(derivatives(separation).values()):
                 far_weights[4 * q : 4 * q + 4, :] = value
 
-            pl.semaphore_wait(barrier, deep - 1 + plane - 1)
-            send_ghosts(step)
-            lax.fori_loop(1, deep, send_column, 0)
         else:
             for k in range(3):
-                place(0, k, coords[k] + centre[k])
-            send_blocks(0)
+                place(placer_start, start_flat, k, coords[k] + centre[k])
+            for b in range(tall):
+                for a in range(wide):
+                    start_out[b, a] = start_flat[8 * (wide * b + a) : 8 * (wide * b + a) + 8, :]
+            for d in range(1, tall):
+                start_y_copy(d).start()
+            for a in range(wide):
+                start_mid[a, gy] = start_out[gy, a]
 
         all_column(step).wait_recv()
         total = message[step, 0]
@@ -439,11 +449,8 @@
         message[step, 1] = total
         plane_in[step, rank] = total
 
-        def send_plane(d, c):
+        for d in others:
             plane_copy(step, d).start()
-            return c
-
-        lax.fori_loop(1, plane, send_plane, 0)
 
         for j in range(6):
 
@@ -485,7 +492,13 @@
                 )
             return c
 
-        lax.fori_loop(0, NPAIR // UNROLL, near, 0)
+        lax.fori_loop(0, NPAIR // UNROLL // 2, near, 0)
+        if step == 1:
+            all_start_y().wait_recv()
+            for d in range(1, wide):
+                start_x_copy(d).start()
+            start_in[gx] = start_mid[gx]
+        lax.fori_loop(NPAIR // UNROLL // 2, NPAIR // UNROLL, near, 0)
         velocity = []
         for k in range(3):
             rows = contrib[pl.ds(3 + k, NPAIR, stride=16), :] + contrib[pl.ds(11 + k, NPAIR, stride=16), :]
@@ -521,16 +534,15 @@
                 own[pl.ds(k, TILES, stride=8), :] = coords[k] + time_step * velocity[k]
 
     for k in range(3):
-        place(1, k, velocity[k])
-    send_blocks(1)
-    all_blocks(0).wait_recv()
-    all_blocks(1).wait_recv()
-    for which, out in ((0, out_start), (1, out_speed)):
-        for k in range(3):
-            for r in range(CAP):
-                rows = pl.ds(which * plane * 8 + 3 * r + k, plane, stride=8)
-                out[k, pl.ds(r, plane, stride=CAP), :] = block_in[rows, :]
-
+        place(placer_speed, speed_out, k, velocity[k])
+
+    for d in others:
+        speed_copy(d).start()
+    speed_in[speed_rows(rank), :] = speed_out[speed_rows(rank), :]
+    all_start_x().wait_recv()
+    for a in range(wide):
+        for b in range(tall):
+            start_flat[8 * (tall * a + b) : 8 * (tall * a + b) + 8, :] = start_in[a, b]
     for step in range(2):
         for j in range(6):
 
@@ -540,7 +552,14 @@
 
         all_column(step).wait_send()
         all_plane(step).wait_send()
-        all_blocks(step).wait_send()
+    all_start_y().wait_send()
+    all_start_x().wait_send()
+    all_speed().wait_recv()
+    for held, out in ((start_flat, out_start), (speed_in, out_speed)):
+        for k in range(3):
+            for r in range(CAP):
+                out[k, pl.ds(r, plane, stride=CAP), :] = held[pl.ds(3 * r + k, plane, stride=8), :]
+    all_speed().wait_send()
 
 
 def finish(start, speed):
@@ -584,16 +603,20 @@
             pltpu.VMEM((MESSAGE, plane), f32),
             pltpu.VMEM((4 * COUNT, LANES), f32),
             pltpu.VMEM((4 * COUNT, plane), f32),
-            pltpu.VMEM((2 * plane * 8, LANES), f32),
-            pltpu.VMEM((2 * plane * 8, LANES), f32),
+            pltpu.VMEM((plane * 8, LANES), f32),
+            pltpu.VMEM((tall, wide, 8, LANES), f32),
+            pltpu.VMEM((wide, tall, 8, LANES), f32),
+            pltpu.VMEM((wide, tall, 8, LANES), f32),
+            pltpu.VMEM((plane * 8, LANES), f32),
+            pltpu.VMEM((plane * 8, LANES), f32),
             dma((2, 6)),
             dma((2, 6)),
             dma((2,)),
             dma((2,)),
             dma((2,)),
             dma((2,)),
-            dma((2,)),
-            dma((2,)),
+            dma((3,)),
+            dma((3,)),
         ],
         compiler_params=pltpu.CompilerParams(
             collective_id=0, has_side_effects=True, vmem_limit_bytes=62 << 20

time: 42.4 us -> 40.1 us (0.946)
  Pallas kernels: 39.1 us -> 36.9 us
    pallas_call x1, Pallas kernels: 39.1 us -> 36.9 us  [per_device(): pl.pallas_call(functools.partial(kernel, sizes), out_shape=(shape, shape)...]
where the time goes in v2:
time: 40.1 us; the launch traced here: 39.9 us
  Pallas kernels  36.9 us (92%)
  other arithmetic  1.63 us (4%)
  between operations  0.65 us (2%)
  local copies, waits for them, and re-layouts  0.64 us (2%)
    pallas_call x1, Pallas kernels, per_device(): pl.pallas_call(functools.partial(kernel, sizes), out_shape=(shape, shape)...  36.9 us
    transpose x1, other arithmetic, finish(): return (moved.transpose(1, 0, 2), speed.transpose(1, 0, 2))  1.63 us

profile of v2, /device:TPU:1, one launch (start us, length us, event | category | flops | bytes accessed | tf_op | source)
XLA Modules:
  0.0 39.9 jit_solution(12570682240595266457)
XLA Ops:
  0.6 36.9 %dislocation_steps.1 = (f32[3,64,128]{2,1,0:T(8,128)}, f32[3,64,128]{2,1,0:T(8,128)}) custom-call(f32[3,4096]{1,0:T(4,128)} %offsets_in.1, f32[3,4096]{1,0:T(4,128)} %strength_in.1, s32[1536]{0:T(1024)} %ghost_list.1, s32[128]{0:T(128)} %target_row.1, s32[128]{0:T(128)} %target_row.1, s32[128]{0:T(128)} %sources.1, s32[1,32]{1,0:T(1,128)} %bitcast.5), custom_call_target="tpu_custom_call" | custom-call | tf_op jit(solution)/shard_map/dislocation_steps/pallas_call | solution.py:579
  37.6 0.0 copy-start
  37.6 1.6 %add_bitcast_fusion = f32[64,3,128]{2,0,1:T(8,128)} fusion(f32[3,64,128]{2,1,0:T(8,128)} %get-tuple-element.4, f32[3,64,128]{2,1,0:T(8,128)} %get-tuple-element.5), kind=kLoop, calls=%fused_computation | loop fusion | flops 49152 | bytes 294912 | tf_op jit(solution)/shard_map/transpose | solution.py:567
  39.2 0.0 copy-done
  39.2 0.6 %copy.9 = f32[64,3,128]{2,0,1:T(8,128)} copy(f32[64,3,128]{2,0,1:T(8,128)S(1)} %bitcast.4) | data formatting | bytes 196608
Async XLA Ops:
  37.6 1.6 %copy-start = (f32[3,64,128]{2,1,0:T(8,128)S(1)}, f32[3,64,128]{2,1,0:T(8,128)}, u32[]{:S(2)}) copy-start(f32[3,64,128]{2,1,0:T(8,128)} %get-tuple-element.5) | copy-start | bytes 294916

commit v3 on v2

--- a/solution.py
+++ b/solution.py
@@ -95,7 +95,7 @@
 def kernel(
     sizes,
     offsets_in, strength_in, ghost_list, targets, target_row, sources, owners,
-    out_start, out_speed,
+    out_pos, out_vel,
     offsets, strength, input_done,
     own, paired, ghost_out, ghost_in, ghost_out_late, ghost_in_late, target_feat, source_feat, source_str, contrib, partial,
     message, column_in, plane_in, gathered, turned, local, far_weights,
@@ -220,21 +220,21 @@
     def start_y_copy(d):
         target = along_y(d)
         return remote(
-            start_out.at[target[1]], start_mid.at[:, gy], block_send.at[1], block_recv.at[1], target
+            start_out.at[target[1], :, pl.ds(0, 3 * CAP)], start_mid.at[:, gy, pl.ds(0, 3 * CAP)], block_send.at[1], block_recv.at[1], target
         )
 
     def all_start_y():
-        part = start_mid.at[:, pl.ds(0, tall - 1)]
+        part = start_mid.at[:, pl.ds(0, tall - 1), pl.ds(0, 3 * CAP)]
         return remote(part, part, block_send.at[1], block_recv.at[1], along_y(1))
 
     def start_x_copy(d):
         target = along_x(d)
         return remote(
-            start_mid.at[target[0]], start_in.at[gx], block_send.at[2], block_recv.at[2], target
+            start_mid.at[target[0], :, pl.ds(0, 3 * CAP)], start_in.at[gx, :, pl.ds(0, 3 * CAP)], block_send.at[2], block_recv.at[2], target
         )
 
     def all_start_x():
-        part = start_in.at[pl.ds(0, wide - 1)]
+        part = start_in.at[pl.ds(0, wide - 1), :, pl.ds(0, 3 * CAP)]
         return remote(part, part, block_send.at[2], block_recv.at[2], along_x(1))
 
     def ghost_copy(step, j):
@@ -555,16 +555,36 @@
     all_start_y().wait_send()
     all_start_x().wait_send()
     all_speed().wait_recv()
-    for held, out in ((start_flat, out_start), (speed_in, out_speed)):
-        for k in range(3):
-            for r in range(CAP):
-                out[k, pl.ds(r, plane, stride=CAP), :] = held[pl.ds(3 * r + k, plane, stride=8), :]
+    for k in range(3):
+        for r in range(CAP):
+            held = pl.ds(3 * r + k, plane, stride=8)
+            slot = pl.ds(r, plane, stride=CAP)
+            out_vel[k, slot, :] = speed_in[held, :]
+            out_pos[k, slot, :] = start_flat[held, :] + time_step * speed_in[held, :]
     all_speed().wait_send()
 
 
-def finish(start, speed):
-    moved = start + time_step * speed
-    return moved.transpose(1, 0, 2), speed.transpose(1, 0, 2)
+def hand_on(pos_in, vel_in, pos_out, vel_out, done):
+    first = pltpu.make_async_copy(pos_in, pos_out, done.at[0])
+    second = pltpu.make_async_copy(vel_in, vel_out, done.at[1])
+    first.start()
+    second.start()
+    first.wait()
+    second.wait()
+
+
+def finish(positions, velocity):
+    hbm = pl.BlockSpec(memory_space=pltpu.HBM)
+    vmem = pl.BlockSpec(memory_space=pltpu.VMEM)
+    positions, velocity = pl.pallas_call(
+        hand_on,
+        out_shape=tuple(jax.ShapeDtypeStruct(a.shape, a.dtype) for a in (positions, velocity)),
+        in_specs=[vmem, vmem],
+        out_specs=(hbm, hbm),
+        scratch_shapes=[pltpu.SemaphoreType.DMA((2,))],
+        name="hand_on",
+    )(positions, velocity)
+    return positions.transpose(1, 0, 2), velocity.transpose(1, 0, 2)
 
 
 def per_device(offsets, strength, ghost_list, pair_targets, pair_sources, owners):
@@ -576,7 +596,7 @@
     hbm = pl.BlockSpec(memory_space=pltpu.HBM)
     shape = jax.ShapeDtypeStruct((3, plane * CAP, LANES), f32)
     dma = pltpu.SemaphoreType.DMA
-    start, speed = pl.pallas_call(
+    positions, velocity = pl.pallas_call(
         functools.partial(kernel, sizes),
         out_shape=(shape, shape),
         in_specs=[hbm, hbm, vmem, smem, vmem, smem, vmem],
@@ -623,7 +643,7 @@
         ),
         name="dislocation_steps",
     )(offsets, strength, ghost_list, pair_targets, pair_targets, pair_sources, owners.reshape(1, TILES))
-    return finish(start, speed)
+    return finish(positions, velocity)
 
 
 def solution(mesh):

time: 40.1 us -> 39.1 us (0.975)
  other arithmetic: 1.63 us -> 0 us
  Pallas kernels: 36.9 us -> 38.2 us
  local copies, waits for them, and re-layouts: 0.64 us -> 0 us
    pallas_call x0 -> x1, Pallas kernels: none -> 1.63 us  [finish(): pl.pallas_call(hand_on, out_shape=tuple((jax.ShapeDtypeStruct(a.shape, a....]
    transpose x1 -> x0, other arithmetic: 1.63 us -> none  [finish(): return (moved.transpose(1, 0, 2), speed.transpose(1, 0, 2))]
    unnamed x3 -> x0, local copies, waits for them, and re-layouts: 0.64 us -> none
where the time goes in v3:
time: 39.1 us; the launch traced here: 38.9 us
  Pallas kernels  38.2 us (98%)
  between operations  0.64 us (2%)
    pallas_call x1, Pallas kernels, per_device(): pl.pallas_call(functools.partial(kernel, sizes), out_shape=(shape, shape)...  36.6 us
    pallas_call x1, Pallas kernels, finish(): pl.pallas_call(hand_on, out_shape=tuple((jax.ShapeDtypeStruct(a.shape, a....  1.63 us

profile of v3, /device:TPU:1, one launch (start us, length us, event | category | flops | bytes accessed | tf_op | source)
XLA Modules:
  0.0 38.9 jit_solution(133276170406610744)
XLA Ops:
  0.6 36.6 %dislocation_steps.1 = (f32[3,64,128]{2,1,0:T(8,128)}, f32[3,64,128]{2,1,0:T(8,128)}) custom-call(f32[3,4096]{1,0:T(4,128)} %offsets_in.1, f32[3,4096]{1,0:T(4,128)} %strength_in.1, s32[1536]{0:T(1024)} %ghost_list.1, s32[128]{0:T(128)} %target_row.1, s32[128]{0:T(128)} %target_row.1, s32[128]{0:T(128)} %sources.1, s32[1,32]{1,0:T(1,128)} %bitcast.3), custom_call_target="tpu_custom_call" | custom-call | tf_op jit(solution)/shard_map/dislocation_steps/pallas_call | solution.py:599
  37.3 1.6 %hand_on.1 = (f32[3,64,128]{2,1,0:T(8,128)}, f32[3,64,128]{2,1,0:T(8,128)}) custom-call(f32[3,64,128]{2,1,0:T(8,128)} %get-tuple-element.6.pos_in, f32[3,64,128]{2,1,0:T(8,128)} %get-tuple-element.7.vel_in), custom_call_target="tpu_custom_call" | custom-call | tf_op jit(solution)/shard_map/hand_on/pallas_call | solution.py:579

commit v4 on v3

--- a/solution.py
+++ b/solution.py
@@ -151,7 +151,6 @@
 
     scale = jnp.where(lax.broadcasted_iota(jnp.int32, (3, LANES), 0) == 2, side, 1.0)
     own[...] = jnp.zeros_like(own)
-    target_feat[...] = jnp.zeros_like(target_feat)
     start_flat[...] = jnp.zeros_like(start_flat)
     speed_out[...] = jnp.zeros_like(speed_out)
     load_offsets.wait()
@@ -420,6 +419,8 @@
                     source_str[t] = strength_rows(raw)
             source_quad(q, tiles)
 
+        if step == 0:
+            target_feat[...] = jnp.zeros_like(target_feat)
         lax.fori_loop(0, TILES // 16, own_quads, 0)
 
         if step == 0:

time: 39.1 us -> 39.1 us (level)
  no operation moved by 1% of the time
where the time goes in v4:
time: 39.1 us; the launch traced here: 38.9 us
  Pallas kernels  38.2 us (98%)
  between operations  0.64 us (2%)
    pallas_call x1, Pallas kernels, per_device(): pl.pallas_call(functools.partial(kernel, sizes), out_shape=(shape, shape)...  36.6 us
    pallas_call x1, Pallas kernels, finish(): pl.pallas_call(hand_on, out_shape=tuple((jax.ShapeDtypeStruct(a.shape, a....  1.63 us

profile of v4, /device:TPU:1, one launch (start us, length us, event | category | flops | bytes accessed | tf_op | source)
XLA Modules:
  0.0 38.9 jit_solution(1968556778749931427)
XLA Ops:
  0.6 36.6 %dislocation_steps.1 = (f32[3,64,128]{2,1,0:T(8,128)}, f32[3,64,128]{2,1,0:T(8,128)}) custom-call(f32[3,4096]{1,0:T(4,128)} %offsets_in.1, f32[3,4096]{1,0:T(4,128)} %strength_in.1, s32[1536]{0:T(1024)} %ghost_list.1, s32[128]{0:T(128)} %target_row.1, s32[128]{0:T(128)} %target_row.1, s32[128]{0:T(128)} %sources.1, s32[1,32]{1,0:T(1,128)} %bitcast.3), custom_call_target="tpu_custom_call" | custom-call | tf_op jit(solution)/shard_map/dislocation_steps/pallas_call | solution.py:600
  37.2 1.6 %hand_on.1 = (f32[3,64,128]{2,1,0:T(8,128)}, f32[3,64,128]{2,1,0:T(8,128)}) custom-call(f32[3,64,128]{2,1,0:T(8,128)} %get-tuple-element.6.pos_in, f32[3,64,128]{2,1,0:T(8,128)} %get-tuple-element.7.vel_in), custom_call_target="tpu_custom_call" | custom-call | tf_op jit(solution)/shard_map/hand_on/pallas_call | solution.py:580
